TPU v7x, 32 devices: a whole 2x2x4 slice. The times are simulated.
32 devices in a mesh: rows: 8 (over z, y), snaps: 4 (over x, core).
Axes of the slice: x: 2, y: 2, z: 4, core: 2. Of those that a mesh axis runs over, the one named last changes fastest.
Arguments:
- stress: float32 [131072, 1024], P('rows', 'snaps'), may hold values from -80 to 80
- sketch: float32 [64, 1024], P(None, 'snaps'), may hold values from -0.1875 to 0.1875
Outputs:
- basis: float32 [64, 131072], P(None, ('rows', 'snaps'))
- coeffs: float32 [64, 1024], P(None, 'snaps')
- spectrum: float32 [64, 64], replicated
All inputs are finite; a program needn't handle non-finite values.
Results may differ from a plain program's by a relative error of at most 0.0015.
Values sent between devices are 32-bit elements; how exact they have to be, the bound alone decides.
A program may use at most 128 MiB of HBM per device.

v0:
```python
import math
import jax
import jax.numpy as jnp
from jax import lax
from jax.sharding import PartitionSpec as P


def product(left_m, right_m, left_dim, right_dim):
    return lax.dot_general(
        left_m,
        right_m,
        (((left_dim,), (right_dim,)), ((), ())),
        precision=lax.Precision.HIGHEST,
        preferred_element_type=jnp.float32,
    )


def inverse_factor(gram_total):
    lower = jnp.linalg.cholesky(gram_total)
    ident = jnp.eye(gram_total.shape[0], dtype=gram_total.dtype)
    return lax.linalg.triangular_solve(lower, ident, left_side=True, lower=True)


def section_whole(panel, stress):
    factor = inverse_factor(lax.psum(product(panel, panel, 1, 1), "rows"))
    basis = product(factor, panel, 1, 0)
    coeffs = lax.psum(product(basis, stress, 1, 0), "rows")
    return (basis, coeffs)


def on_device(stress, sketch):
    rows_dev = stress.shape[0]
    groups = lax.axis_size("snaps")
    share = rows_dev // groups
    operand = sketch
    basis = None
    for turn in range(2):
        partial_value = product(operand, stress, 1, 1)
        panel = lax.psum(partial_value, "snaps")
        basis, operand = section_whole(panel, stress)
    basis = lax.dynamic_slice_in_dim(basis, lax.axis_index("snaps") * share, share, 1)
    scale = math.sqrt(float(rows_dev * lax.axis_size("rows")))
    batch_total = operand.shape[1] * groups
    spectrum = lax.psum(product(operand, operand, 1, 1), "snaps") / batch_total
    return (basis * scale, operand, spectrum)


def solution(mesh):
    placed = (P("rows", "snaps"), P(None, "snaps"))
    return jax.shard_map(
        on_device,
        mesh=mesh,
        in_specs=placed,
        out_specs=(P(None, ("rows", "snaps")), P(None, "snaps"), P()),
        check_vma=False,
    )
```

profile of v0, /device:TPU:0, one launch (start us, length us, event | category | flops | bytes accessed | tf_op | source)
XLA Modules:
  0.0 522.6 jit_solution(17021512674975102727)
XLA Ops:
  7.2 0.8 copy-done
  8.0 20.6 %fusion.12 = f32[64,16384]{1,0:T(8,128)} fusion(f32[64,256]{1,0:T(8,128)S(1)} %copy-done, f32[16384,256]{1,0:T(8,128)} %param.5), kind=kOutput, calls=%fused_computation.23 | convolution fusion | flops 3221225472 | bytes 21037056 | tf_op jit(solution)/shard_map/dot_general | solution.py:9
  28.7 88.3 %all-reduce.5.cloned.1.call-done = f32[64,16384]{1,0:T(8,128)} async-done(((f32[64,16384]{1,0:T(8,128)}), f32[64,16384]{1,0:T(8,128)}) %all-reduce.5.cloned.1.call-update) | async-done | bytes 4194320 | tf_op jit(solution)/shard_map/psum | solution.py:39
  117.0 6.9 %fusion.13 = f32[64,64]{0,1:T(8,128)S(1)} fusion(f32[64,16384]{1,0:T(8,128)} %all-reduce.5.cloned.1.call-done), kind=kOutput, calls=%fused_computation.24 | convolution fusion | flops 805306368 | bytes 4210688 | tf_op jit(solution)/shard_map/dot_general | solution.py:9
  124.0 37.2 %psum.50 = f32[64,64]{0,1:T(8,128)S(1)} all-reduce(f32[64,64]{0,1:T(8,128)S(1)} %fusion.13), channel_id=1, replica_groups=mesh['rows'=8,'snaps'=4] {'rows'}, use_global_device_ids=true, to_apply=%region_1.0 | all-reduce | flops 4096 | bytes 32768 | tf_op jit(solution)/shard_map/psum | solution.py:25
  161.2 5.8 %cholesky.44 = f32[64,64]{1,0:T(8,128)S(1)} custom-call(f32[64,64]{1,0:T(8,128)S(1)} %fusion.9), custom_call_target="Cholesky" | custom-call | tf_op jit(solution)/shard_map/jit(cholesky)/cholesky | solution.py:19
  168.4 4.9 custom-call.6
  173.5 5.5 %fusion.14 = f32[64,16384]{1,0:T(8,128)S(1)} fusion(f32[64,64]{1,0:T(8,128)S(1)} %fusion.2, f32[64,16384]{1,0:T(8,128)} %all-reduce.5.cloned.1.call-done), kind=kOutput, calls=%fused_computation.25 | convolution fusion | flops 805306368 | bytes 8404992 | tf_op jit(solution)/shard_map/dot_general | solution.py:9
  179.0 11.6 %fusion.15 = f32[64,256]{1,0:T(8,128)} fusion(f32[64,16384]{1,0:T(8,128)S(1)} %fusion.14, f32[16384,256]{1,0:T(8,128)} %param.5), kind=kOutput, calls=%fused_computation.26 | convolution fusion | flops 3221225472 | bytes 21037056 | tf_op jit(solution)/shard_map/dot_general | solution.py:9
  190.9 64.8 %all-reduce.7.cloned.1.call-done = f32[64,256]{1,0:T(8,128)} async-done(((f32[64,256]{1,0:T(8,128)}), f32[64,256]{1,0:T(8,128)}) %all-reduce.7.cloned.1.call-update) | async-done | bytes 65552 | tf_op jit(solution)/shard_map/psum | solution.py:27
  255.7 20.6 %fusion.16 = f32[64,16384]{1,0:T(8,128)} fusion(f32[64,256]{1,0:T(8,128)} %all-reduce.7.cloned.1.call-done, f32[16384,256]{1,0:T(8,128)} %param.5), kind=kOutput, calls=%fused_computation.27 | convolution fusion | flops 3221225472 | bytes 21037056 | tf_op jit(solution)/shard_map/dot_general | solution.py:9
  276.4 85.5 %all-reduce.9.cloned.1.call-done = f32[64,16384]{1,0:T(8,128)} async-done(((f32[64,16384]{1,0:T(8,128)}), f32[64,16384]{1,0:T(8,128)}) %all-reduce.9.cloned.1.call-update) | async-done | bytes 4194320 | tf_op jit(solution)/shard_map/psum | solution.py:39
  361.9 6.9 %fusion.17 = f32[64,64]{0,1:T(8,128)S(1)} fusion(f32[64,16384]{1,0:T(8,128)} %all-reduce.9.cloned.1.call-done), kind=kOutput, calls=%fused_computation.28 | convolution fusion | flops 805306368 | bytes 4210688 | tf_op jit(solution)/shard_map/dot_general | solution.py:9
  368.9 37.1 %psum.53 = f32[64,64]{0,1:T(8,128)S(1)} all-reduce(f32[64,64]{0,1:T(8,128)S(1)} %fusion.17), channel_id=1, replica_groups=mesh['rows'=8,'snaps'=4] {'rows'}, use_global_device_ids=true, to_apply=%region_6.9 | all-reduce | flops 4096 | bytes 32768 | tf_op jit(solution)/shard_map/psum | solution.py:25
  406.1 5.8 %cholesky.55 = f32[64,64]{1,0:T(8,128)S(1)} custom-call(f32[64,64]{1,0:T(8,128)S(1)} %fusion.7), custom_call_target="Cholesky" | custom-call | tf_op jit(solution)/shard_map/jit(cholesky)/cholesky | solution.py:19
  413.3 4.9 custom-call.7
  418.5 5.5 %fusion.18 = f32[64,16384]{1,0:T(8,128)S(1)} fusion(f32[64,64]{1,0:T(8,128)S(1)} %fusion, f32[64,16384]{1,0:T(8,128)} %all-reduce.9.cloned.1.call-done), kind=kOutput, calls=%fused_computation.29 | convolution fusion | flops 805306368 | bytes 8404992 | tf_op jit(solution)/shard_map/dot_general | solution.py:9
  423.9 1.9 copy-done.1
  425.9 11.6 %fusion.19 = f32[64,256]{1,0:T(8,128)} fusion(f32[64,16384]{1,0:T(8,128)S(1)} %fusion.18, f32[16384,256]{1,0:T(8,128)} %param.5), kind=kOutput, calls=%fused_computation.30 | convolution fusion | flops 3221225472 | bytes 21037056 | tf_op jit(solution)/shard_map/dot_general | solution.py:9
  437.5 2.3 dynamic-slice_multiply_fusion
  439.8 62.8 %all-reduce.11.cloned.1.call-done = f32[64,256]{1,0:T(8,128)} async-done(((f32[64,256]{1,0:T(8,128)}), f32[64,256]{1,0:T(8,128)}) %all-reduce.11.cloned.1.call-update) | async-done | bytes 65552 | tf_op jit(solution)/shard_map/psum | solution.py:27
  502.5 1.1 fusion.20
  503.7 10.3 %psum.55 = f32[64,64]{1,0:T(8,128)S(1)} all-reduce(f32[64,64]{1,0:T(8,128)S(1)} %fusion.20), channel_id=1, replica_groups=mesh['rows'=8,'snaps'=4] {'snaps'}, use_global_device_ids=true, to_apply=%region_8.11 | all-reduce | flops 4096 | bytes 32768 | tf_op jit(solution)/shard_map/psum | solution.py:44
  514.6 1.5 copy.15
  (23 shorter events, 4.4 us)
Async XLA Ops:
  7.2 0.8 copy-start
  7.2 109.8 %all-reduce.5.cloned.1.call-start = ((), (), s32[]{:S(2)}) async-start(), calls=%async_computation | async-start | bytes 8388608 | tf_op jit(solution)/shard_map/psum | solution.py:39
  28.7 227.1 %all-reduce.7.cloned.1.call-start = ((), (), s32[]{:S(2)}) async-start(), calls=%async_computation.1 | async-start | bytes 131072 | tf_op jit(solution)/shard_map/psum | solution.py:27
  190.6 171.3 %all-reduce.9.cloned.1.call-start = ((), (), s32[]{:S(2)}) async-start(), calls=%async_computation.2 | async-start | bytes 8388608 | tf_op jit(solution)/shard_map/psum | solution.py:39
  276.4 226.2 %all-reduce.11.cloned.1.call-start = ((), (), s32[]{:S(2)}) async-start(), calls=%async_computation.3 | async-start | bytes 131072 | tf_op jit(solution)/shard_map/psum | solution.py:27
  423.9 1.9 copy-start.1
Sparse Core Ops, SparseCore 0:
  28.8 88.1 all-reduce.4
  190.8 64.9 all-reduce.6
  276.5 85.4 all-reduce.8
  437.6 64.9 all-reduce.10
where the time goes:
time: 523 us
  waiting for transfers between devices  301 us (58%)
  matrix products  90.8 us (17%)
  blocking collectives  84.6 us (16%)
  other arithmetic  27.1 us (5%)
  between operations  13.9 us (3%)
    psum x2, waiting for transfers between devices, on_device(): panel = lax.psum(partial_value, 'snaps')  174 us
    psum x2, waiting for transfers between devices, section_whole(): coeffs = lax.psum(product(basis, stress, 1, 0), 'rows')  128 us
    dot_general x9, matrix products, product(): lax.dot_general(left_m, right_m, (((left_dim,), (right_dim,)), ((), ())),...  90.3 us
    psum x2, blocking collectives, section_whole(): factor = inverse_factor(lax.psum(product(panel, panel, 1, 1), 'rows'))  74.3 us
    another operation x6, other arithmetic, inverse_factor(): lower = jnp.linalg.cholesky(gram_total)  13 us
    another operation x4, other arithmetic, inverse_factor(): return lax.linalg.triangular_solve(lower, ident, left_side=True, lower=True)  11.1 us
  transfers between devices with their start and end apart: 4, of which 4 were waited for; matrix products, arithmetic and copies ran while one was open for 0% of the time, Pallas kernels for 0%

commit v1 on v0

--- a/solution.py
+++ b/solution.py
@@ -36,7 +36,7 @@
     basis = None
     for turn in range(2):
         partial_value = product(operand, stress, 1, 1)
-        panel = lax.psum(partial_value, "snaps")
+        panel = jnp.sum(lax.all_gather(partial_value, "snaps"), axis=0)
         basis, operand = section_whole(panel, stress)
     basis = lax.dynamic_slice_in_dim(basis, lax.axis_index("snaps") * share, share, 1)
     scale = math.sqrt(float(rows_dev * lax.axis_size("rows")))

time: 523 us -> 603 us (1.15); the launches traced: 523 us -> 594 us
  waiting for transfers between devices: 301 us -> 342 us
  other arithmetic: 27.1 us -> 45.5 us
  blocking collectives: 84.6 us -> 96.9 us
    all_gather x0 -> x2, waiting for transfers between devices: none -> 215 us  [on_device(): panel = jnp.sum(lax.all_gather(partial_value, 'snaps'), axis=0)]
    psum x2 -> x0, waiting for transfers between devices: 174 us -> none  [on_device(): panel = lax.psum(partial_value, 'snaps')]
    reduce_sum x0 -> x2, other arithmetic: none -> 18.5 us  [on_device(): panel = jnp.sum(lax.all_gather(partial_value, 'snaps'), axis=0)]
    psum x2, blocking collectives: 74.3 us -> 86.7 us  [section_whole(): factor = inverse_factor(lax.psum(product(panel, panel, 1, 1), 'rows'))]
where the time goes in v1:
time: 603 us; the launch traced here: 594 us
  waiting for transfers between devices  342 us (57%)
  blocking collectives  96.9 us (16%)
  matrix products  90.9 us (15%)
  other arithmetic  45.5 us (8%)
  between operations  14.3 us (2%)
    all_gather x2, waiting for transfers between devices, on_device(): panel = jnp.sum(lax.all_gather(partial_value, 'snaps'), axis=0)  215 us
    psum x2, waiting for transfers between devices, section_whole(): coeffs = lax.psum(product(basis, stress, 1, 0), 'rows')  128 us
    dot_general x9, matrix products, product(): lax.dot_general(left_m, right_m, (((left_dim,), (right_dim,)), ((), ())),...  90.4 us
    psum x2, blocking collectives, section_whole(): factor = inverse_factor(lax.psum(product(panel, panel, 1, 1), 'rows'))  86.7 us
    reduce_sum x2, other arithmetic, on_device(): panel = jnp.sum(lax.all_gather(partial_value, 'snaps'), axis=0)  18.5 us
    another operation x6, other arithmetic, inverse_factor(): lower = jnp.linalg.cholesky(gram_total)  13 us
  transfers between devices with their start and end apart: 4, of which 4 were waited for; matrix products, arithmetic and copies ran while one was open for 0% of the time, Pallas kernels for 0%

profile of v1, /device:TPU:0, one launch (start us, length us, event | category | flops | bytes accessed | tf_op | source)
XLA Modules:
  0.0 594.5 jit_solution(1053675495872672289)
XLA Ops:
  8.0 20.6 %fusion.12 = f32[64,16384]{1,0:T(8,128)} fusion(f32[64,256]{1,0:T(8,128)S(1)} %copy-done, f32[16384,256]{1,0:T(8,128)} %param.5), kind=kOutput, calls=%fused_computation.23 | convolution fusion | flops 3221225472 | bytes 21037056 | tf_op jit(solution)/shard_map/dot_general | solution.py:9
  28.7 108.7 %all-gather.5.cloned.1.call-done = f32[256,16384]{1,0:T(8,128)} async-done(((f32[64,16384]{1,0:T(8,128)}), f32[256,16384]{1,0:T(8,128)}) %all-gather.5.cloned.1.call-update) | async-done | bytes 16777232 | tf_op jit(solution)/shard_map/all_gather | solution.py:39
  137.4 9.2 %reduce_sum.18 = f32[64,16384]{1,0:T(8,128)} reduce(f32[4,64,16384]{2,1,0:T(8,128)} %bitcast.39, f32[]{:T(128)} %constant.39.clone.1), dimensions={0}, to_apply=%region_0.0 | reduce | flops 3145728 | bytes 20971524 | tf_op jit(solution)/shard_map/reduce_sum | solution.py:39
  146.7 6.9 %fusion.13 = f32[64,64]{0,1:T(8,128)S(1)} fusion(f32[64,16384]{1,0:T(8,128)} %reduce_sum.18), kind=kOutput, calls=%fused_computation.24 | convolution fusion | flops 805306368 | bytes 4210688 | tf_op jit(solution)/shard_map/dot_general | solution.py:9
  153.6 49.6 %psum.35 = f32[64,64]{0,1:T(8,128)S(1)} all-reduce(f32[64,64]{0,1:T(8,128)S(1)} %fusion.13), channel_id=1, replica_groups=mesh['rows'=8,'snaps'=4] {'rows'}, use_global_device_ids=true, to_apply=%region_1.0 | all-reduce | flops 4096 | bytes 32768 | tf_op jit(solution)/shard_map/psum | solution.py:25
  203.3 5.8 cholesky.44
  210.5 4.9 custom-call.6
  215.6 5.5 fusion.14
  221.1 11.6 %fusion.15 = f32[64,256]{1,0:T(8,128)} fusion(f32[64,16384]{1,0:T(8,128)S(1)} %fusion.14, f32[16384,256]{1,0:T(8,128)} %param.5), kind=kOutput, calls=%fused_computation.26 | convolution fusion | flops 3221225472 | bytes 21037056 | tf_op jit(solution)/shard_map/dot_general | solution.py:9
  232.7 64.9 %all-reduce.3.cloned.1.call-done = f32[64,256]{1,0:T(8,128)} async-done(((f32[64,256]{1,0:T(8,128)}), f32[64,256]{1,0:T(8,128)}) %all-reduce.3.cloned.1.call-update) | async-done | bytes 65552 | tf_op jit(solution)/shard_map/psum | solution.py:27
  297.7 20.6 %fusion.16 = f32[64,16384]{1,0:T(8,128)} fusion(f32[64,256]{1,0:T(8,128)} %all-reduce.3.cloned.1.call-done, f32[16384,256]{1,0:T(8,128)} %param.5), kind=kOutput, calls=%fused_computation.27 | convolution fusion | flops 3221225472 | bytes 21037056 | tf_op jit(solution)/shard_map/dot_general | solution.py:9
  318.4 106.0 %all-gather.7.cloned.1.call-done = f32[256,16384]{1,0:T(8,128)} async-done(((f32[64,16384]{1,0:T(8,128)}), f32[256,16384]{1,0:T(8,128)}) %all-gather.7.cloned.1.call-update) | async-done | bytes 16777232 | tf_op jit(solution)/shard_map/all_gather | solution.py:39
  424.3 9.2 %reduce_sum.19 = f32[64,16384]{1,0:T(8,128)} reduce(f32[4,64,16384]{2,1,0:T(8,128)} %bitcast.38, f32[]{:T(128)} %constant.39.clone.1), dimensions={0}, to_apply=%region_5.8 | reduce | flops 3145728 | bytes 20971524 | tf_op jit(solution)/shard_map/reduce_sum | solution.py:39
  433.5 6.9 %fusion.17 = f32[64,64]{0,1:T(8,128)S(1)} fusion(f32[64,16384]{1,0:T(8,128)} %reduce_sum.19), kind=kOutput, calls=%fused_computation.28 | convolution fusion | flops 805306368 | bytes 4210688 | tf_op jit(solution)/shard_map/dot_general | solution.py:9
  440.5 37.1 %psum.37 = f32[64,64]{0,1:T(8,128)S(1)} all-reduce(f32[64,64]{0,1:T(8,128)S(1)} %fusion.17), channel_id=1, replica_groups=mesh['rows'=8,'snaps'=4] {'rows'}, use_global_device_ids=true, to_apply=%region_6.9 | all-reduce | flops 4096 | bytes 32768 | tf_op jit(solution)/shard_map/psum | solution.py:25
  477.7 5.8 cholesky.55
  484.9 4.9 custom-call.7
  490.1 5.5 fusion.18
  495.5 1.9 copy-done.2
  497.5 11.6 %fusion.19 = f32[64,256]{1,0:T(8,128)} fusion(f32[64,16384]{1,0:T(8,128)S(1)} %fusion.18, f32[16384,256]{1,0:T(8,128)} %param.5), kind=kOutput, calls=%fused_computation.30 | convolution fusion | flops 3221225472 | bytes 21037056 | tf_op jit(solution)/shard_map/dot_general | solution.py:9
  509.1 2.3 dynamic-slice_multiply_fusion
  511.4 62.7 %all-reduce.5.cloned.1.call-done = f32[64,256]{1,0:T(8,128)} async-done(((f32[64,256]{1,0:T(8,128)}), f32[64,256]{1,0:T(8,128)}) %all-reduce.5.cloned.1.call-update) | async-done | bytes 65552 | tf_op jit(solution)/shard_map/psum | solution.py:27
  575.2 10.3 %psum.39 = f32[64,64]{1,0:T(8,128)S(1)} all-reduce(f32[64,64]{1,0:T(8,128)S(1)} %fusion.20), channel_id=1, replica_groups=mesh['rows'=8,'snaps'=4] {'snaps'}, use_global_device_ids=true, to_apply=%region_8.11 | all-reduce | flops 4096 | bytes 32768 | tf_op jit(solution)/shard_map/psum | solution.py:44
  586.1 1.5 copy.13
  (27 shorter events, 6.1 us)
Async XLA Ops:
  7.2 0.8 copy-start
  7.2 130.3 %all-gather.5.cloned.1.call-start = ((), (), s32[]{:S(2)}) async-start(), calls=%async_computation.2 | async-start | bytes 20971520 | tf_op jit(solution)/shard_map/all_gather | solution.py:39
  28.7 269.0 %all-reduce.3.cloned.1.call-start = ((), (), s32[]{:S(2)}) async-start(), calls=%async_computation | async-start | bytes 131072 | tf_op jit(solution)/shard_map/psum | solution.py:27
  232.7 191.6 %all-gather.7.cloned.1.call-start = ((), (), s32[]{:S(2)}) async-start(), calls=%async_computation.3 | async-start | bytes 20971520 | tf_op jit(solution)/shard_map/all_gather | solution.py:39
  318.3 255.8 %all-reduce.5.cloned.1.call-start = ((), (), s32[]{:S(2)}) async-start(), calls=%async_computation.1 | async-start | bytes 131072 | tf_op jit(solution)/shard_map/psum | solution.py:27
  495.5 1.9 copy-start.2
  497.5 90.1 %copy-start.1 = (f32[64,256]{1,0:T(8,128)S(1)}, f32[64,256]{1,0:T(8,128)}, u32[]{:S(2)}) copy-start(f32[64,256]{1,0:T(8,128)} %param.6) | copy-start | bytes 196612
Sparse Core Ops, SparseCore 0:
  28.8 108.6 all-gather.4
  232.8 64.7 all-reduce.2
  318.4 105.8 all-gather.6
  509.2 64.8 all-reduce.4
